TPU v7x, 32 devices: a whole 2x2x4 slice. The times are simulated.
32 devices in a mesh: groups: 2 (over y), param: 4 (over z), dp: 4 (over x, core).
Axes of the slice: x: 2, y: 2, z: 4, core: 2. Of those that a mesh axis runs over, the one named last changes fastest.
Arguments:
- acts: bfloat16 [8, 4096, 8192], P('groups', 'dp', 'param'), parts along dimension 0, may hold values from -6 to 6
- grads: bfloat16 [8, 4096, 16384], P('groups', 'dp', 'param'), parts along dimension 0, may hold values from -6 to 6
- lengths: int32 [8], P('groups'), parts along dimension 0, may hold values from 1024 to 4096, as said below
- row_sign: int32 [8192], P('param'), may hold values from 0 to 1
- col_sign: int32 [16384], P('param'), may hold values from 0 to 1
- row_index: int32 [64], replicated, may hold values from 0 to 8191
- col_index: int32 [128], replicated, may hold values from 0 to 16383
Outputs:
- sketch: float32 [8, 64, 128], P('groups', 'param', 'dp'), parts along dimension 0
There are 2 independent parts, one for each index of `groups`. A program takes and returns all parts, laid end to end along the dimension named above; an argument that names none is the same for every part. Nothing has to cross between parts.
Inputs may be any that keep to these rules, and one draw needn't show every extreme that they name: `lengths`: some example has all 4096 tokens live.
All inputs are finite; a program needn't handle non-finite values.
Results may differ from a plain program's by a relative error of at most 0.0003.
Values sent between devices are 32-bit elements; how exact they have to be, the bound alone decides.
A program may use at most 128 MiB of HBM per device.

v0:
```python
import jax
import jax.numpy as jnp
from jax import lax
from jax.sharding import PartitionSpec as P

D = 8192
F = 16384


def bit_parity(values):
    folded = values
    for shift in (16, 8, 4, 2, 1):
        folded = jnp.bitwise_xor(folded, jnp.right_shift(folded, shift))
    return jnp.bitwise_and(folded, 1)


def hadamard_block(indices, offset, width):
    columns = offset + jnp.arange(width, dtype=jnp.int32)
    parity = bit_parity(jnp.bitwise_and(columns[:, None], indices[None, :]))
    return (1 - 2 * parity).astype(jnp.bfloat16)


def local(acts, grads, lengths, row_sign, col_sign, row_index, col_index):
    tok_block = acts.shape[1]
    row_block = acts.shape[2]
    col_block = grads.shape[2]
    param_pos = lax.axis_index("param")
    data_pos = lax.axis_index("dp")
    data_count = lax.axis_size("dp")
    position = data_pos * tok_block + jnp.arange(tok_block, dtype=jnp.int32)
    live = position[None, :] < lengths[:, None]
    row_flip = (1 - 2 * row_sign).astype(jnp.bfloat16)
    col_flip = (1 - 2 * col_sign).astype(jnp.bfloat16)
    masked = jnp.where(
        live[:, :, None], acts * row_flip[None, None, :], jnp.zeros((), jnp.bfloat16)
    )
    flipped = grads * col_flip[None, None, :]
    row_table = hadamard_block(row_index, param_pos * row_block, row_block)
    col_table = hadamard_block(col_index, param_pos * col_block, col_block)
    rows_term = jnp.einsum("etd,dk->etk", masked, row_table, preferred_element_type=jnp.float32) * (
        1.0 / D**0.5
    )
    cols_term = jnp.einsum(
        "etd,dk->etk", flipped, col_table, preferred_element_type=jnp.float32
    ) * (1.0 / F**0.5)
    final_scale = 1.0 / (tok_block * data_count) ** 0.5
    rows_mixed = lax.psum(rows_term, "param")
    partial_sketch = jnp.einsum(
        "etk,etl->ekl", rows_mixed, cols_term, precision=lax.Precision.HIGHEST
    )
    partial_sketch = lax.psum_scatter(partial_sketch, "param", scatter_dimension=1, tiled=True)
    summed = lax.psum_scatter(partial_sketch, "dp", scatter_dimension=2, tiled=True)
    return summed * final_scale


def solution(mesh):
    placed = (
        P("groups", "dp", "param"),
        P("groups", "dp", "param"),
        P("groups"),
        P("param"),
        P("param"),
        P(),
        P(),
    )
    return jax.shard_map(
        local, mesh=mesh, in_specs=placed, out_specs=P("groups", "param", "dp"), check_vma=False
    )
```

profile of v0, /device:TPU:0, one launch (start us, length us, event | category | flops | bytes accessed | tf_op | source)
XLA Modules:
  0.0 122.6 jit_solution(359580122624809772)
XLA Ops:
  6.5 0.0 all-reduce.2.cloned.1.call-start
  6.5 0.7 broadcast_compare_fusion
  7.3 0.7 iota_add_fusion.1
  8.0 0.0 copy-start
  8.0 0.0 copy-start.1
  8.0 9.8 %fusion.15 = f32[4,1024,64]{1,2,0:T(8,128)} fusion(bf16[4,1024,2048]{2,1,0:T(8,128)(2,1)} %param.7, pred[4,1024]{1,0:T(4,128)(4,1)S(1)} %broadcast_compare_fusion, bf16[2048]{0:T(1024)(128)(2,1)S(1)} %get-tuple-element.6, s32[64]{0:T(128)} %param.12, s32[2048]{0:T(1024)S(1)} %get-tuple-element.5), kind=kOutput, calls=%fused_computation.20 | convolution fusion | flops 1092747264 | bytes 17842432 | tf_op jit(solution)/shard_map/etd,dk->etk/dot_general | solution.py:40
  17.8 0.0 all-reduce.2.cloned.1.call-update
  17.8 0.0 reduce-scatter.5.cloned.1.call-start
  17.9 0.0 copy-done
  17.9 0.0 copy-done.1
  17.9 14.7 %fusion = f32[4,1024,128]{2,1,0:T(8,128)S(1)} fusion(bf16[4,1024,4096]{2,1,0:T(8,128)(2,1)} %param.8, bf16[4096]{0:T(1024)(128)(2,1)S(1)} %get-tuple-element.8, s32[128]{0:T(128)S(1)} %copy-done.1, s32[4096]{0:T(1024)S(1)} %get-tuple-element.7), kind=kOutput, calls=%fused_computation | convolution fusion | flops 4319608832 | bytes 35676672 | tf_op jit(solution)/shard_map/etd,dk->etk/dot_general | solution.py:43
  32.6 39.9 %all-reduce.2.cloned.1.call-done = f32[4,1024,64]{1,2,0:T(8,128)} async-done(((f32[4,1024,64]{1,2,0:T(8,128)}), f32[4,1024,64]{1,2,0:T(8,128)}) %all-reduce.2.cloned.1.call-update) | async-done | bytes 1048592 | tf_op jit(solution)/shard_map/psum | solution.py:47
  72.5 3.3 %fusion.12 = f32[4,64,128]{2,1,0:T(8,128)} fusion(f32[4,1024,64]{1,2,0:T(8,128)} %all-reduce.2.cloned.1.call-done, f32[4,1024,128]{2,1,0:T(8,128)S(1)} %fusion), kind=kOutput, calls=%fused_computation.17 | convolution fusion | flops 403177472 | bytes 3276800 | tf_op jit(solution)/shard_map/etk,etl->ekl/dot_general | solution.py:48
  75.8 0.0 reduce-scatter.5.cloned.1.call-update
  75.8 0.0 reduce-scatter.7.cloned.1.call-start
  75.8 18.7 %reduce-scatter.5.cloned.1.call-done = f32[4,16,128]{2,1,0:T(8,128)} async-done(((f32[4,64,128]{2,1,0:T(8,128)}), f32[4,16,128]{2,1,0:T(8,128)}) %reduce-scatter.5.cloned.1.call-update) | async-done | bytes 32784 | tf_op jit(solution)/shard_map/reduce_scatter | solution.py:51
  94.5 0.9 copy.8
  95.4 0.8 reshape.46
  96.2 0.0 reduce-scatter.7.cloned.1.call-update
  96.2 18.4 %reduce-scatter.7.cloned.1.call-done = f32[32,64]{1,0:T(8,128)} async-done(((f32[128,64]{1,0:T(8,128)}), f32[32,64]{1,0:T(8,128)}) %reduce-scatter.7.cloned.1.call-update) | async-done | bytes 8208
  114.6 0.8 reshape.47
  115.4 0.1 copy.9
  115.5 0.6 broadcast_multiply_fusion
  (2 shorter events, 0.0 us)
Async XLA Ops:
  6.5 66.0 %all-reduce.2.cloned.1.call-start = ((), (), s32[]{:S(2)}) async-start(), calls=%async_computation.2 | async-start | bytes 2097152 | tf_op jit(solution)/shard_map/psum | solution.py:47
  8.0 9.9 %copy-start = (s32[4096]{0:T(1024)S(1)}, s32[4096]{0:T(1024)}, u32[]{:S(2)}) copy-start(s32[4096]{0:T(1024)} %param.11) | copy-start | bytes 49156
  8.0 9.9 %copy-start.1 = (s32[128]{0:T(128)S(1)}, s32[128]{0:T(128)}, u32[]{:S(2)}) copy-start(s32[128]{0:T(128)} %param.13) | copy-start | bytes 1540
  17.8 76.7 %reduce-scatter.5.cloned.1.call-start = ((), (), s32[]{:S(2)}) async-start(), calls=%async_computation.3 | async-start | bytes 163840 | tf_op jit(solution)/shard_map/reduce_scatter | solution.py:51
  75.8 38.8 %reduce-scatter.7.cloned.1.call-start = ((), (), s32[]{:S(2)}) async-start(), calls=%async_computation.4 | async-start | bytes 81920
Sparse Core Ops, SparseCore 0:
  17.9 54.5 all-reduce.1
  75.9 18.5 reduce-scatter.4
  96.9 17.6 reduce-scatter.6
where the time goes:
time: 123 us
  waiting for transfers between devices  77 us (63%)
  matrix products  27.8 us (23%)
  between operations  13.2 us (11%)
  local copies, waits for them, and re-layouts  2.57 us (2%)
  other arithmetic  2.07 us (2%)
    psum x1, waiting for transfers between devices, local(): rows_mixed = lax.psum(rows_term, 'param')  39.9 us
    reduce_scatter x1, waiting for transfers between devices, local(): lax.psum_scatter(partial_sketch, 'param', scatter_dimension=1, tiled=True)  18.7 us
    unnamed x4, waiting for transfers between devices  18.4 us
    dot_general x1, matrix products, local(): jnp.einsum('etd,dk->etk', flipped, col_table, preferred_element_type=jnp....  14.7 us
    dot_general x1, matrix products, local(): jnp.einsum('etd,dk->etk', masked, row_table, preferred_element_type=jnp.f...  9.81 us
    dot_general x1, matrix products, local(): jnp.einsum('etk,etl->ekl', rows_mixed, cols_term, precision=lax.Precision...  3.28 us
    unnamed x8, local copies, waits for them, and re-layouts  2.57 us
  transfers between devices with their start and end apart: 3, of which 3 were waited for; matrix products, arithmetic and copies ran while one was open for 12% of the time, Pallas kernels for 0%

commit v1 on v0

v1 whole, which is shorter than its diff:
```python
import functools

import jax
import jax.numpy as jnp
from jax import lax
from jax.experimental import pallas as pl
from jax.experimental.pallas import tpu as pltpu
from jax.sharding import PartitionSpec as P

D = 8192
F = 16384
BLK = 512
HALF = BLK // 2
SUB = HALF // 2
LAG = 2
SLOTS = 4


def signed_table(indices, sign, offset, width):
    columns = offset + jnp.arange(width, dtype=jnp.int32)
    bits = lax.population_count(jnp.bitwise_and(columns[:, None], indices[None, :]))
    parity = jnp.bitwise_and(bits + sign[:, None], 1)
    return (1 - 2 * parity).astype(jnp.bfloat16)


def split(x):
    hi = x.astype(jnp.bfloat16)
    return hi, (x - hi.astype(jnp.float32)).astype(jnp.bfloat16)


def dot(a, b):
    return jnp.dot(a, b, preferred_element_type=jnp.float32)


def kernel(zn, dn, scale, lengths, rtab, ctab, acts, grads, out, abuf, gbuf, own, pin, sin,
           pout, sout, chi, clo, acc, part, part_in, ybuf, zbuf, zin, asem, gsem, psend, precv,
           ssend, srecv, dsend, drecv, zsend, zrecv):
    z = lax.axis_index("param")
    d = lax.axis_index("dp")
    examples, tokens, _ = acts.shape
    per = tokens // BLK
    blocks = examples * per
    chunks = 2 * blocks
    tail = LAG * (zn - 1) // 2
    cm = part.shape[2]
    rm = zbuf.shape[1]
    ka = 64

    def fetch(src, buf, sem, j):
        slot = lax.rem(j, SLOTS)
        rows = pl.ds(pl.multiple_of(lax.rem(j, per) * BLK, BLK), BLK)
        return pltpu.make_async_copy(src.at[j // per, rows, :], buf.at[slot], sem.at[slot])

    for j in range(min(SLOTS, blocks)):
        fetch(acts, abuf, asem, jnp.int32(j)).start()
        fetch(grads, gbuf, gsem, jnp.int32(j)).start()

    barrier = pltpu.get_barrier_semaphore()
    for off in range(1, zn):
        pl.semaphore_signal(barrier, inc=1, device_id={"param": lax.rem(z + off, zn)},
                            device_id_type=pl.DeviceIdType.MESH)
    for off in range(1, dn):
        pl.semaphore_signal(barrier, inc=1, device_id={"dp": lax.rem(d + off, dn)},
                            device_id_type=pl.DeviceIdType.MESH)
    pl.semaphore_wait(barrier, zn - 1 + dn - 1)

    def up(k):
        return pltpu.make_async_remote_copy(
            src_ref=pout.at[k], dst_ref=pin.at[k], send_sem=psend.at[k], recv_sem=precv.at[k],
            device_id={"param": lax.rem(z + 1, zn)}, device_id_type=pl.DeviceIdType.MESH)

    def down(k):
        return pltpu.make_async_remote_copy(
            src_ref=sout.at[k], dst_ref=sin.at[k], send_sem=ssend.at[k], recv_sem=srecv.at[k],
            device_id={"param": lax.rem(z + zn - 1, zn)}, device_id_type=pl.DeviceIdType.MESH)

    def across(e, off):
        peer = lax.rem(d + off, dn)
        return pltpu.make_async_remote_copy(
            src_ref=part.at[e, peer], dst_ref=part_in.at[e, off - 1],
            send_sem=dsend.at[e, off - 1], recv_sem=drecv.at[e, off - 1],
            device_id={"dp": peer}, device_id_type=pl.DeviceIdType.MESH)

    def along(off):
        peer = lax.rem(z + off, zn)
        return pltpu.make_async_remote_copy(
            src_ref=zbuf.at[peer], dst_ref=zin.at[off - 1],
            send_sem=zsend.at[off - 1], recv_sem=zrecv.at[off - 1],
            device_id={"param": peer}, device_id_type=pl.DeviceIdType.MESH)

    def one_way(t, place, copy, arrived, leaving):
        k = t - LAG * place

        @pl.when(jnp.logical_and(k >= 0, k < chunks))
        def _():
            @pl.when(place > 0)
            def _():
                copy(k).wait_recv()

            @pl.when(place == 0)
            def _():
                arrived[k] = jnp.zeros((SUB, 128), jnp.float32)

            @pl.when(place < zn - 1)
            def _():
                leaving[k] = own[k] + arrived[k]
                copy(k).start()

    def exchange(t):
        one_way(t, z, up, pin, pout)
        one_way(t, zn - 1 - z, down, sin, sout)

    lane = lax.broadcasted_iota(jnp.int32, (HALF, 128), 1)
    row = lax.broadcasted_iota(jnp.int32, (HALF, 128), 0)
    place = d * tokens + row + jnp.where(lane >= ka, HALF, 0)

    def step(j, carry):
        @pl.when(j < blocks)
        def _():
            slot = lax.rem(j, SLOTS)
            fetch(acts, abuf, asem, j).wait()
            value = dot(abuf[slot, :HALF, :], rtab[:, :128])
            value = value + dot(abuf[slot, HALF:, :], rtab[:, 128:])
            live = place + lax.rem(j, per) * BLK < lengths[j // per]
            value = jnp.where(live, value, 0.0)
            own[2 * j] = value[:SUB]
            own[2 * j + 1] = value[SUB:]

            @pl.when(j + SLOTS < blocks)
            def _():
                fetch(acts, abuf, asem, j + SLOTS).start()

        exchange(2 * j)

        @pl.when(j < blocks)
        def _():
            slot = lax.rem(j, SLOTS)
            fetch(grads, gbuf, gsem, j).wait()
            for half in range(2):
                value = dot(gbuf[slot, half * HALF:(half + 1) * HALF, :], ctab[...])
                hi, lo = split(value.T)
                chi[j, half * 128:(half + 1) * 128, :] = hi
                clo[j, half * 128:(half + 1) * 128, :] = lo

            @pl.when(j + SLOTS < blocks)
            def _():
                fetch(grads, gbuf, gsem, j + SLOTS).start()

        exchange(2 * j + 1)

        @pl.when(j >= tail)
        def _():
            b = j - tail
            e = b // per
            h = lax.rem(b, per)
            total = jnp.concatenate(
                [own[2 * b + s] + pin[2 * b + s] + sin[2 * b + s] for s in range(2)], axis=0)
            hi, lo = split(total)
            value = dot(chi[b], hi) + (dot(chi[b], lo) + dot(clo[b], hi))

            @pl.when(h == 0)
            def _():
                acc[...] = value

            @pl.when(h > 0)
            def _():
                acc[...] += value

            @pl.when(h == per - 1)
            def _():
                lanes = lax.broadcasted_iota(jnp.int32, (128, 128), 1)
                both = jnp.where(lanes < ka, acc[:128, :], acc[128:, :])
                for p in range(dn):
                    part[e, p] = both[p * cm:(p + 1) * cm]
                for off in range(1, dn):
                    across(e, off).start()

        return carry

    lax.fori_loop(0, blocks + tail, step, 0)

    for e in range(examples):
        value = part[e, d]
        for off in range(1, dn):
            across(e, off).wait_recv()
            value = value + part_in[e, off - 1]
        ybuf[e * cm:(e + 1) * cm, :] = value
    turned = ybuf[...].T
    turned = turned[:ka] + turned[ka:]
    for p in range(zn):
        zbuf[p] = turned[p * rm:(p + 1) * rm]
    for off in range(1, zn):
        along(off).start()
    value = zbuf[z]
    for off in range(1, zn):
        along(off).wait_recv()
        value = value + zin[off - 1]
    value = value * scale
    for e in range(examples):
        out[e] = value[:, e * cm:(e + 1) * cm]

    for off in range(1, zn):
        along(off).wait_send()
    for e in range(examples):
        for off in range(1, dn):
            across(e, off).wait_send()

    def drain(k, carry):
        @pl.when(z < zn - 1)
        def _():
            up(k).wait_send()

        @pl.when(z > 0)
        def _():
            down(k).wait_send()

        return carry

    lax.fori_loop(0, chunks, drain, 0)


def local(acts, grads, lengths, row_sign, col_sign, row_index, col_index):
    examples, tokens, row_block = acts.shape
    col_block = grads.shape[2]
    z = lax.axis_index("param")
    zn = lax.axis_size("param")
    dn = lax.axis_size("dp")
    ka = row_index.shape[0]
    kb = col_index.shape[0]
    rm, cm = ka // zn, kb // dn
    rows = signed_table(row_index, row_sign, z * row_block, row_block)
    none = jnp.zeros_like(rows)
    rtab = jnp.concatenate([rows, none, none, rows], axis=1)
    ctab = signed_table(col_index, col_sign, z * col_block, col_block)
    scale = 1.0 / (D**0.5 * F**0.5 * (tokens * dn) ** 0.5)
    blocks = examples * tokens // BLK
    line = pltpu.VMEM((2 * blocks, SUB, 128), jnp.float32)
    dma = pltpu.SemaphoreType.DMA
    vmem = pl.BlockSpec(memory_space=pltpu.VMEM)
    hbm = pl.BlockSpec(memory_space=pl.ANY)
    return pl.pallas_call(
        functools.partial(kernel, zn, dn, scale),
        out_shape=jax.ShapeDtypeStruct((examples, rm, cm), jnp.float32),
        in_specs=[pl.BlockSpec(memory_space=pltpu.SMEM), vmem, vmem, hbm, hbm],
        out_specs=vmem,
        scratch_shapes=[
            pltpu.VMEM((SLOTS, BLK, row_block), jnp.bfloat16),
            pltpu.VMEM((SLOTS, BLK, col_block), jnp.bfloat16),
            line, line, line, line, line,
            pltpu.VMEM((blocks, 256, HALF), jnp.bfloat16),
            pltpu.VMEM((blocks, 256, HALF), jnp.bfloat16),
            pltpu.VMEM((256, 128), jnp.float32),
            pltpu.VMEM((examples, dn, cm, 128), jnp.float32),
            pltpu.VMEM((examples, dn - 1, cm, 128), jnp.float32),
            pltpu.VMEM((examples * cm, 128), jnp.float32),
            pltpu.VMEM((zn, rm, examples * cm), jnp.float32),
            pltpu.VMEM((zn - 1, rm, examples * cm), jnp.float32),
            dma((SLOTS,)), dma((SLOTS,)),
            dma((2 * blocks,)), dma((2 * blocks,)), dma((2 * blocks,)), dma((2 * blocks,)),
            dma((examples, dn - 1)), dma((examples, dn - 1)),
            dma((zn - 1,)), dma((zn - 1,)),
        ],
        compiler_params=pltpu.CompilerParams(
            collective_id=0, has_side_effects=True, vmem_limit_bytes=52 * 1024 * 1024
        ),
        cost_estimate=pl.CostEstimate(
            flops=2 * examples * tokens * (row_block * ka + col_block * kb),
            bytes_accessed=2 * examples * tokens * (row_block + col_block),
            transcendentals=0,
        ),
    )(lengths, rtab, ctab, acts, grads)


def solution(mesh):
    placed = (
        P("groups", "dp", "param"),
        P("groups", "dp", "param"),
        P("groups"),
        P("param"),
        P("param"),
        P(),
        P(),
    )
    return jax.shard_map(
        local, mesh=mesh, in_specs=placed, out_specs=P("groups", "param", "dp"), check_vma=False
    )
```

time: 123 us -> 58.2 us (0.47)
  waiting for transfers between devices: 77 us -> 0 us
  Pallas kernels: 0 us -> 51.9 us
  matrix products: 27.8 us -> 0 us
  between operations: 13.2 us -> 0.05 us
  other arithmetic: 2.07 us -> 5.36 us
  local copies, waits for them, and re-layouts: 2.57 us -> 0.71 us
    pallas_call x0 -> x1, Pallas kernels: none -> 51.9 us  [local(): pl.pallas_call(functools.partial(kernel, zn, dn, scale), out_shape=jax.Sh...]
    psum x1 -> x0, waiting for transfers between devices: 39.9 us -> none  [local(): rows_mixed = lax.psum(rows_term, 'param')]
    dot_general x3 -> x0, matrix products: 27.8 us -> none  [the longest x1 14.7 us: local(): jnp.einsum('etd,dk->etk', flipped, col_table, preferred_element_type=jnp....]
    reduce_scatter x1 -> x0, waiting for transfers between devices: 18.7 us -> none  [local(): lax.psum_scatter(partial_sketch, 'param', scatter_dimension=1, tiled=True)]
    unnamed x4 -> x0, waiting for transfers between devices: 18.4 us -> none
    convert_element_type x0 -> x2, other arithmetic: none -> 5.02 us  [signed_table(): return (1 - 2 * parity).astype(jnp.bfloat16)]
    unnamed x8 -> x7, local copies, waits for them, and re-layouts: 2.57 us -> 0.63 us
  transfers between devices with their start and end apart: 3 -> 0, of which waited for: 3 -> 0; matrix products, arithmetic and copies ran while one was open for 12% -> 0% of each run, Pallas kernels for 0% -> 0%
where the time goes in v1:
time: 58.2 us; the launch traced here: 58 us
  Pallas kernels  51.9 us (89%)
  other arithmetic  5.36 us (9%)
  local copies, waits for them, and re-layouts  0.71 us (1%)
    pallas_call x1, Pallas kernels, local(): pl.pallas_call(functools.partial(kernel, zn, dn, scale), out_shape=jax.Sh...  51.9 us
    convert_element_type x2, other arithmetic, signed_table(): return (1 - 2 * parity).astype(jnp.bfloat16)  5.02 us

profile of v1, /device:TPU:0, one launch (start us, length us, event | category | flops | bytes accessed | tf_op | source)
XLA Modules:
  0.0 58.0 jit_solution(9703129797659791727)
XLA Ops:
  0.0 0.0 copy-start.2
  0.0 0.0 copy-start.1
  0.0 0.0 copy-start
  0.0 0.1 pad.1.clone
  0.1 2.6 %subtract_convert_fusion.1 = bf16[2048,64]{1,0:T(8,128)(2,1)S(1)} fusion(s32[2048]{0:T(1024)} %param.10, s32[64]{0:T(128)} %param.12, s32[2048]{0:T(1024)S(1)} %iota_add_fusion.1), kind=kLoop, calls=%fused_computation.2 | loop fusion | flops 917504 | bytes 278784 | tf_op jit(solution)/shard_map/convert_element_type | solution.py:23
  2.7 0.3 pad_maximum_fusion.rtab
  3.0 0.0 copy-done.2
  3.0 0.0 copy-done.1
  3.0 2.5 %subtract_convert_fusion.ctab = bf16[4096,128]{1,0:T(8,128)(2,1)} fusion(s32[4096]{0:T(1024)S(1)} %copy-done.1, s32[128]{0:T(128)S(1)} %copy-done.2, s32[4096]{0:T(1024)S(1)} %iota_add_fusion), kind=kLoop, calls=%fused_computation | loop fusion | flops 3670016 | bytes 1081856 | tf_op jit(solution)/shard_map/convert_element_type | solution.py:23
  5.5 0.0 copy-done
  5.5 51.9 %shard_map.73 = f32[4,16,32]{2,1,0:T(8,128)S(1)} custom-call(s32[4]{0:T(128)S(1)} %copy-done, bf16[2048,256]{1,0:T(8,128)(2,1)S(1)} %pad_maximum_fusion.rtab, bf16[4096,128]{1,0:T(8,128)(2,1)} %subtract_convert_fusion.ctab, bf16[4,1024,2048]{2,1,0:T(8,128)(2,1)} %acts.1, bf16[4,1024,4096]{2,1,0:T(8,128)(2,1)} %grads.1), custom_call_target="tpu_custom_call" | custom-call | flops 5368709120 | bytes 50331648 | tf_op jit(solution)/shard_map/pallas_call | solution.py:241
  57.4 0.6 %copy.11 = f32[4,16,32]{2,1,0:T(8,128)} copy(f32[4,16,32]{2,1,0:T(8,128)S(1)} %shard_map.73) | data formatting | bytes 16384
  (3 shorter events, 0.0 us)
Async XLA Ops:
  0.0 3.0 %copy-start.2 = (s32[128]{0:T(128)S(1)}, s32[128]{0:T(128)}, u32[]{:S(2)}) copy-start(s32[128]{0:T(128)} %param.13) | copy-start | bytes 1540
  0.0 3.0 %copy-start.1 = (s32[4096]{0:T(1024)S(1)}, s32[4096]{0:T(1024)}, u32[]{:S(2)}) copy-start(s32[4096]{0:T(1024)} %param.11) | copy-start | bytes 49156
  0.0 5.5 %copy-start = (s32[4]{0:T(128)S(1)}, s32[4]{0:T(128)}, u32[]{:S(2)}) copy-start(s32[4]{0:T(128)} %lengths.1) | copy-start | bytes 52

commit v2 on v1

--- a/solution.py
+++ b/solution.py
@@ -12,15 +12,16 @@
 BLK = 512
 HALF = BLK // 2
 SUB = HALF // 2
-LAG = 2
+LAG = 3
 SLOTS = 4
 
 
-def signed_table(indices, sign, offset, width):
-    columns = offset + jnp.arange(width, dtype=jnp.int32)
-    bits = lax.population_count(jnp.bitwise_and(columns[:, None], indices[None, :]))
-    parity = jnp.bitwise_and(bits + sign[:, None], 1)
-    return (1 - 2 * parity).astype(jnp.bfloat16)
+def hadamard_signs(base, stride, count, index):
+    values = base + stride * lax.broadcasted_iota(jnp.int32, (count, 128), 0)
+    values = jnp.bitwise_and(values, index)
+    for shift in (16, 8, 4, 2, 1):
+        values = jnp.bitwise_xor(values, jnp.right_shift(values, shift))
+    return (1 - 2 * jnp.bitwise_and(values, 1)).astype(jnp.float32)
 
 
 def split(x):
@@ -32,7 +33,7 @@
     return jnp.dot(a, b, preferred_element_type=jnp.float32)
 
 
-def kernel(zn, dn, scale, lengths, rtab, ctab, acts, grads, out, abuf, gbuf, own, pin, sin,
+def kernel(zn, dn, scale, lengths, rsign, csign, rindex, cindex, acts, grads, out, rtab, ctab, abuf, gbuf, own, pin, sin,
            pout, sout, chi, clo, acc, part, part_in, ybuf, zbuf, zin, asem, gsem, psend, precv,
            ssend, srecv, dsend, drecv, zsend, zrecv):
     z = lax.axis_index("param")
@@ -41,7 +42,7 @@
     per = tokens // BLK
     blocks = examples * per
     chunks = 2 * blocks
-    tail = LAG * (zn - 1) // 2
+    tail = (LAG * (zn - 1) + 1) // 2
     cm = part.shape[2]
     rm = zbuf.shape[1]
     ka = 64
@@ -62,6 +63,22 @@
     for off in range(1, dn):
         pl.semaphore_signal(barrier, inc=1, device_id={"dp": lax.rem(d + off, dn)},
                             device_id_type=pl.DeviceIdType.MESH)
+    def fill(sign, index, store):
+        groups = sign.shape[0]
+        high = hadamard_signs(z * groups * 128, 128, groups, index[...])
+        low = hadamard_signs(0, 1, 128, index[...])
+        flips = (1 - 2 * sign[...]).astype(jnp.float32).T
+        for g in range(groups):
+            store(g * 128, (low * high[g:g + 1, :]) * flips[:, g:g + 1])
+
+    def store_rows(at, value):
+        rtab[at:at + 128, :] = value.astype(jnp.bfloat16)
+
+    def store_cols(at, value):
+        ctab[at:at + 128, :] = value.astype(jnp.bfloat16)
+
+    fill(rsign, rindex, store_rows)
+    fill(csign, cindex, store_cols)
     pl.semaphore_wait(barrier, zn - 1 + dn - 1)
 
     def up(k):
@@ -119,8 +136,9 @@
         def _():
             slot = lax.rem(j, SLOTS)
             fetch(acts, abuf, asem, j).wait()
-            value = dot(abuf[slot, :HALF, :], rtab[:, :128])
-            value = value + dot(abuf[slot, HALF:, :], rtab[:, 128:])
+            value = jnp.where(
+                lane < ka, dot(abuf[slot, :HALF, :], rtab[...]), dot(abuf[slot, HALF:, :], rtab[...])
+            )
             live = place + lax.rem(j, per) * BLK < lengths[j // per]
             value = jnp.where(live, value, 0.0)
             own[2 * j] = value[:SUB]
@@ -222,16 +240,11 @@
 def local(acts, grads, lengths, row_sign, col_sign, row_index, col_index):
     examples, tokens, row_block = acts.shape
     col_block = grads.shape[2]
-    z = lax.axis_index("param")
     zn = lax.axis_size("param")
     dn = lax.axis_size("dp")
     ka = row_index.shape[0]
     kb = col_index.shape[0]
     rm, cm = ka // zn, kb // dn
-    rows = signed_table(row_index, row_sign, z * row_block, row_block)
-    none = jnp.zeros_like(rows)
-    rtab = jnp.concatenate([rows, none, none, rows], axis=1)
-    ctab = signed_table(col_index, col_sign, z * col_block, col_block)
     scale = 1.0 / (D**0.5 * F**0.5 * (tokens * dn) ** 0.5)
     blocks = examples * tokens // BLK
     line = pltpu.VMEM((2 * blocks, SUB, 128), jnp.float32)
@@ -241,9 +254,11 @@
     return pl.pallas_call(
         functools.partial(kernel, zn, dn, scale),
         out_shape=jax.ShapeDtypeStruct((examples, rm, cm), jnp.float32),
-        in_specs=[pl.BlockSpec(memory_space=pltpu.SMEM), vmem, vmem, hbm, hbm],
+        in_specs=[pl.BlockSpec(memory_space=pltpu.SMEM), vmem, vmem, vmem, vmem, hbm, hbm],
         out_specs=vmem,
         scratch_shapes=[
+            pltpu.VMEM((row_block, 128), jnp.bfloat16),
+            pltpu.VMEM((col_block, kb), jnp.bfloat16),
             pltpu.VMEM((SLOTS, BLK, row_block), jnp.bfloat16),
             pltpu.VMEM((SLOTS, BLK, col_block), jnp.bfloat16),
             line, line, line, line, line,
@@ -268,7 +283,15 @@
             bytes_accessed=2 * examples * tokens * (row_block + col_block),
             transcendentals=0,
         ),
-    )(lengths, rtab, ctab, acts, grads)
+    )(
+        lengths,
+        row_sign.reshape(-1, 128),
+        col_sign.reshape(-1, 128),
+        jnp.concatenate([row_index] * (128 // ka)).reshape(1, 128),
+        col_index.reshape(1, 128),
+        acts,
+        grads,
+    )
 
 
 def solution(mesh):

time: 58.2 us -> 50.9 us (0.87)
  Pallas kernels: 51.9 us -> 46.4 us
  other arithmetic: 5.36 us -> 0.8 us
  local copies, waits for them, and re-layouts: 0.71 us -> 3.34 us
    pallas_call x1, Pallas kernels: 51.9 us -> 46.4 us  [local(): pl.pallas_call(functools.partial(kernel, zn, dn, scale), out_shape=jax.Sh...]
    convert_element_type x2 -> x0, other arithmetic: 5.02 us -> none  [signed_table(): return (1 - 2 * parity).astype(jnp.bfloat16)]
    unnamed x7 -> x9, local copies, waits for them, and re-layouts: 0.63 us -> 3.34 us
    reshape x0 -> x1, other arithmetic: none -> 0.8 us  [local(): jnp.concatenate([row_index] * (128 // ka)).reshape(1, 128)]
where the time goes in v2:
time: 50.9 us; the launch traced here: 50.6 us
  Pallas kernels  46.4 us (91%)
  local copies, waits for them, and re-layouts  3.34 us (7%)
  other arithmetic  0.8 us (2%)
    pallas_call x1, Pallas kernels, local(): pl.pallas_call(functools.partial(kernel, zn, dn, scale), out_shape=jax.Sh...  46.4 us
    unnamed x9, local copies, waits for them, and re-layouts  3.34 us

profile of v2, /device:TPU:0, one launch (start us, length us, event | category | flops | bytes accessed | tf_op | source)
XLA Modules:
  0.0 50.6 jit_solution(11797036462083107128)
XLA Ops:
  0.0 0.8 %add_bitcast_fusion.rindex = s32[1,128]{1,0:T(1,128)S(1)} fusion(s32[64]{0:T(128)} %param.12), kind=kLoop, calls=%fused_computation | loop fusion | flops 128 | bytes 768 | tf_op jit(solution)/shard_map/reshape | solution.py:290
  0.8 0.0 copy-start
  0.8 0.7 %copy-done = s32[4096]{0:T(1024)S(1)} copy-done((s32[4096]{0:T(1024)S(1)}, s32[4096]{0:T(1024)}, u32[]{:S(2)}) %copy-start) | copy-done | bytes 16408
  1.5 0.0 copy-start.1
  1.5 0.7 %copy-done.1 = s32[2048]{0:T(1024)S(1)} copy-done((s32[2048]{0:T(1024)S(1)}, s32[2048]{0:T(1024)}, u32[]{:S(2)}) %copy-start.1) | copy-done | bytes 8216
  2.2 0.0 copy-start.2
  2.2 0.7 %copy-done.2 = s32[4]{0:T(128)S(1)} copy-done((s32[4]{0:T(128)S(1)}, s32[4]{0:T(128)}, u32[]{:S(2)}) %copy-start.2) | copy-done | bytes 40
  2.9 0.0 copy-start.3
  2.9 0.7 %copy-done.3 = s32[128]{0:T(128)S(1)} copy-done((s32[128]{0:T(128)S(1)}, s32[128]{0:T(128)}, u32[]{:S(2)}) %copy-start.3) | copy-done | bytes 536
  3.5 46.4 %shard_map.73 = f32[4,16,32]{2,1,0:T(8,128)S(1)} custom-call(s32[4]{0:T(128)S(1)} %copy-done.2, s32[16,128]{1,0:T(8,128)S(1)} %bitcast.6, s32[32,128]{1,0:T(8,128)S(1)} %bitcast.5, s32[1,128]{1,0:T(1,128)S(1)} %add_bitcast_fusion.rindex, s32[1,128]{1,0:T(1,128)S(1)} %bitcast.7, bf16[4,1024,2048]{2,1,0:T(8,128)(2,1)} %acts.1, bf16[4,1024,4096]{2,1,0:T(8,128)(2,1)} %grads.1), custom_call_target="tpu_custom_call" | custom-call | flops 5368709120 | bytes 50331648 | tf_op jit(solution)/shard_map/pallas_call | solution.py:254
  50.0 0.6 %copy.9 = f32[4,16,32]{2,1,0:T(8,128)} copy(f32[4,16,32]{2,1,0:T(8,128)S(1)} %shard_map.73) | data formatting | bytes 16384
Async XLA Ops:
  0.8 0.7 %copy-start = (s32[4096]{0:T(1024)S(1)}, s32[4096]{0:T(1024)}, u32[]{:S(2)}) copy-start(s32[4096]{0:T(1024)} %param.11) | copy-start | bytes 49156
  1.5 0.7 %copy-start.1 = (s32[2048]{0:T(1024)S(1)}, s32[2048]{0:T(1024)}, u32[]{:S(2)}) copy-start(s32[2048]{0:T(1024)} %param.10) | copy-start | bytes 24580
  2.2 0.7 %copy-start.2 = (s32[4]{0:T(128)S(1)}, s32[4]{0:T(128)}, u32[]{:S(2)}) copy-start(s32[4]{0:T(128)} %lengths.1) | copy-start | bytes 52
  2.9 0.7 %copy-start.3 = (s32[128]{0:T(128)S(1)}, s32[128]{0:T(128)}, u32[]{:S(2)}) copy-start(s32[128]{0:T(128)} %param.13) | copy-start | bytes 1540

commit v3 on v2

--- a/solution.py
+++ b/solution.py
@@ -14,6 +14,7 @@
 SUB = HALF // 2
 LAG = 3
 SLOTS = 4
+DELAY = 2
 
 
 def hadamard_signs(base, stride, count, index):
@@ -43,6 +44,7 @@
     blocks = examples * per
     chunks = 2 * blocks
     tail = (LAG * (zn - 1) + 1) // 2
+    delay = min(tail, DELAY)
     cm = part.shape[2]
     rm = zbuf.shape[1]
     ka = 64
@@ -150,19 +152,21 @@
 
         exchange(2 * j)
 
-        @pl.when(j < blocks)
-        def _():
-            slot = lax.rem(j, SLOTS)
-            fetch(grads, gbuf, gsem, j).wait()
+        c = j - delay
+
+        @pl.when(jnp.logical_and(c >= 0, c < blocks))
+        def _():
+            slot = lax.rem(c, SLOTS)
+            fetch(grads, gbuf, gsem, c).wait()
             for half in range(2):
                 value = dot(gbuf[slot, half * HALF:(half + 1) * HALF, :], ctab[...])
                 hi, lo = split(value.T)
-                chi[j, half * 128:(half + 1) * 128, :] = hi
-                clo[j, half * 128:(half + 1) * 128, :] = lo
-
-            @pl.when(j + SLOTS < blocks)
-            def _():
-                fetch(grads, gbuf, gsem, j + SLOTS).start()
+                chi[c, half * 128:(half + 1) * 128, :] = hi
+                clo[c, half * 128:(half + 1) * 128, :] = lo
+
+            @pl.when(c + SLOTS < blocks)
+            def _():
+                fetch(grads, gbuf, gsem, c + SLOTS).start()
 
         exchange(2 * j + 1)
 

time: 50.9 us -> 50.6 us (level)
  no operation moved by 1% of the time
where the time goes in v3:
time: 50.6 us; the launch traced here: 50.3 us
  Pallas kernels  46.1 us (91%)
  local copies, waits for them, and re-layouts  3.34 us (7%)
  other arithmetic  0.8 us (2%)
    pallas_call x1, Pallas kernels, local(): pl.pallas_call(functools.partial(kernel, zn, dn, scale), out_shape=jax.Sh...  46.1 us
    unnamed x9, local copies, waits for them, and re-layouts  3.34 us

profile of v3, /device:TPU:0, one launch (start us, length us, event | category | flops | bytes accessed | tf_op | source)
XLA Modules:
  0.0 50.3 jit_solution(17971318439182803396)
XLA Ops:
  0.0 0.8 %add_bitcast_fusion.rindex = s32[1,128]{1,0:T(1,128)S(1)} fusion(s32[64]{0:T(128)} %param.12), kind=kLoop, calls=%fused_computation | loop fusion | flops 128 | bytes 768 | tf_op jit(solution)/shard_map/reshape | solution.py:294
  0.8 0.0 copy-start
  0.8 0.7 %copy-done = s32[4096]{0:T(1024)S(1)} copy-done((s32[4096]{0:T(1024)S(1)}, s32[4096]{0:T(1024)}, u32[]{:S(2)}) %copy-start) | copy-done | bytes 16408
  1.5 0.0 copy-start.1
  1.5 0.7 %copy-done.1 = s32[2048]{0:T(1024)S(1)} copy-done((s32[2048]{0:T(1024)S(1)}, s32[2048]{0:T(1024)}, u32[]{:S(2)}) %copy-start.1) | copy-done | bytes 8216
  2.2 0.0 copy-start.2
  2.2 0.7 %copy-done.2 = s32[4]{0:T(128)S(1)} copy-done((s32[4]{0:T(128)S(1)}, s32[4]{0:T(128)}, u32[]{:S(2)}) %copy-start.2) | copy-done | bytes 40
  2.9 0.0 copy-start.3
  2.9 0.7 %copy-done.3 = s32[128]{0:T(128)S(1)} copy-done((s32[128]{0:T(128)S(1)}, s32[128]{0:T(128)}, u32[]{:S(2)}) %copy-start.3) | copy-done | bytes 536
  3.5 46.1 %shard_map.73 = f32[4,16,32]{2,1,0:T(8,128)S(1)} custom-call(s32[4]{0:T(128)S(1)} %copy-done.2, s32[16,128]{1,0:T(8,128)S(1)} %bitcast.6, s32[32,128]{1,0:T(8,128)S(1)} %bitcast.5, s32[1,128]{1,0:T(1,128)S(1)} %add_bitcast_fusion.rindex, s32[1,128]{1,0:T(1,128)S(1)} %bitcast.7, bf16[4,1024,2048]{2,1,0:T(8,128)(2,1)} %acts.1, bf16[4,1024,4096]{2,1,0:T(8,128)(2,1)} %grads.1), custom_call_target="tpu_custom_call" | custom-call | flops 5368709120 | bytes 50331648 | tf_op jit(solution)/shard_map/pallas_call | solution.py:258
  49.7 0.6 %copy.9 = f32[4,16,32]{2,1,0:T(8,128)} copy(f32[4,16,32]{2,1,0:T(8,128)S(1)} %shard_map.73) | data formatting | bytes 16384
Async XLA Ops:
  0.8 0.7 %copy-start = (s32[4096]{0:T(1024)S(1)}, s32[4096]{0:T(1024)}, u32[]{:S(2)}) copy-start(s32[4096]{0:T(1024)} %param.11) | copy-start | bytes 49156
  1.5 0.7 %copy-start.1 = (s32[2048]{0:T(1024)S(1)}, s32[2048]{0:T(1024)}, u32[]{:S(2)}) copy-start(s32[2048]{0:T(1024)} %param.10) | copy-start | bytes 24580
  2.2 0.7 %copy-start.2 = (s32[4]{0:T(128)S(1)}, s32[4]{0:T(128)}, u32[]{:S(2)}) copy-start(s32[4]{0:T(128)} %lengths.1) | copy-start | bytes 52
  2.9 0.7 %copy-start.3 = (s32[128]{0:T(128)S(1)}, s32[128]{0:T(128)}, u32[]{:S(2)}) copy-start(s32[128]{0:T(128)} %param.13) | copy-start | bytes 1540
